TPU v7x, 32 devices: a whole 2x2x4 slice. The times are simulated.
32 devices in a mesh: seq: 4 (over y, x), tp: 8 (over z, core).
Axes of the slice: x: 2, y: 2, z: 4, core: 2. Of those that a mesh axis runs over, the one named last changes fastest.
Arguments:
- hidden_in: bfloat16 [24, 4, 1024], P('tp'), may hold values from -6 to 6
- new_query: bfloat16 [24, 4, 1024], P('tp'), may hold values from -70 to 70
- new_key: bfloat16 [24, 4, 1024], P('tp'), may hold values from -15 to 15
- new_value: bfloat16 [24, 4, 1024], P('tp'), may hold values from -6 to 6
- key_cache: bfloat16 [24, 4096, 1024], P('tp', 'seq'), may hold values from -16 to 16
- value_cache: bfloat16 [24, 4096, 1024], P('tp', 'seq'), may hold values from -6 to 6
- lengths: int32 [24], P('tp'), may hold values from 64 to 4096, as said below
- out_weight: bfloat16 [1024, 1024], replicated, may hold values from -0.1875 to 0.1875
- norm_gain: float32 [1024], replicated, may hold values from 0.5 to 1.5
- router_weight: bfloat16 [1024, 16], replicated, may hold values from -0.1875 to 0.1875
- expert_ids: int32 [24, 4, 2], P('tp'), may hold values from 0 to 15, all different within a row
- gate_weight: bfloat16 [45056, 1024], P(('seq', 'tp')), may hold values from -0.1875 to 0.1875
- up_weight: bfloat16 [45056, 1024], P(('seq', 'tp')), may hold values from -0.1875 to 0.1875
- down_weight: bfloat16 [45056, 1024], P(('seq', 'tp')), may hold values from -0.109375 to 0.109375
Outputs:
- attn_out: bfloat16 [24, 4, 1024], P('tp', None, 'seq')
- layer_out: bfloat16 [24, 4, 1024], P('tp', None, 'seq')
Inputs may be any that keep to these rules, and one draw needn't show every extreme that they name: `lengths`: each length is 4096 or between 64 and 128; some request has 4096.
All inputs are finite; a program needn't handle non-finite values.
Results may differ from a plain program's by a relative error of at most 0.014.
Values may be sent and summed in bfloat16 or wider, within the bound.
No kernel may reach another device: no remote copies, remote signals or barrier semaphores. Data moves between devices by JAX's collectives and lax.ppermute only.
A program may use at most 64 MiB of HBM per device.

v0:
```python
import functools

import jax
import jax.numpy as jnp
from jax import lax
from jax.experimental import pallas as pl
from jax.experimental.pallas import tpu as pltpu
from jax.sharding import PartitionSpec as P

HEADS = 16
SHORT = 128
ROWS = 16
LANES = 128
masked_score = -1e30
norm_epsilon = 1e-06
NT = (((1,), (1,)), ((), ()))
TN = (((0,), (0,)), ((), ()))


def iota(shape, dim):
    return lax.broadcasted_iota(jnp.int32, shape, dim)


def over(x, n):
    if n & (n - 1) == 0:
        return lax.shift_right_logical(x, jnp.int32(n.bit_length() - 1))
    return x // n


def within(x, n):
    if n & (n - 1) == 0:
        return x & (n - 1)
    return x % n


def three_parts(x):
    hi = x.astype(jnp.bfloat16).astype(jnp.float32)
    mid = (x - hi).astype(jnp.bfloat16).astype(jnp.float32)
    return hi, mid, x - hi - mid


def tiled(x, times):
    return jnp.concatenate([x] * times, axis=0)


def attend(
    lens_hbm, q_hbm, nk_hbm, nv_hbm, k_hbm, v_hbm, out_ref, fresh_ref,
    lens, q_ref, nk_ref, nv_ref, query_ref, kbuf, vbuf, sems, small_sems,
):
    requests, block, width = k_hbm.shape
    steps = q_ref.shape[1]
    head = width // HEADS
    scale = head ** (-0.5)
    group = 256 // head
    chunks = width // 256
    rows = group * steps
    seq = lax.axis_index("seq")
    small = [
        pltpu.make_async_copy(src, dst, small_sems.at[i])
        for i, (src, dst) in enumerate(
            ((lens_hbm, lens), (q_hbm, q_ref), (nk_hbm, nk_ref), (nv_hbm, nv_ref))
        )
    ]
    for move in small:
        move.start()
    small[0].wait()

    def left(r):
        return lens[r] - seq * block

    def is_full(r):
        return left(r) >= block

    def is_short(r):
        return (left(r) > 0) & (left(r) < block)

    def move(which, r, count):
        src, dst = ((k_hbm, kbuf), (v_hbm, vbuf))[which]
        part = pl.ds(0, count)
        return pltpu.make_async_copy(src.at[r, part], dst.at[r, part], sems.at[which, r])

    for kind, count in ((is_short, SHORT), (is_full, block)):
        for r in range(requests):

            @pl.when(kind(r))
            def _():
                for which in range(2):
                    move(which, r, count).start()

    for move_small in small[1:]:
        move_small.wait()
    diag = over(iota((rows, 256), 0), steps) == over(iota((rows, 256), 1), head)
    diag_all = jnp.concatenate([diag] * chunks, axis=1)
    all_rows = chunks * rows

    def columns(c):
        return slice(c * 256, (c + 1) * 256)

    def against(query, keys):
        return jnp.concatenate(
            [
                lax.dot_general(
                    query[:, columns(c)], keys(c), NT, preferred_element_type=jnp.float32
                )
                for c in range(chunks)
            ],
            axis=0,
        )

    def summary(top, total):
        shape = (all_rows, LANES)
        part = over(iota(shape, 1), HEADS)
        spread = jnp.zeros(shape, jnp.float32)
        for place, value in enumerate(three_parts(top) + three_parts(total)):
            spread = jnp.where(part == place, value, spread)
        spread = jnp.where(
            within(iota(shape, 1), HEADS) == over(iota(shape, 0), steps), spread, 0.0
        )
        pick = within(iota((ROWS, all_rows), 1), steps) == iota((ROWS, all_rows), 0)
        gathered = jnp.dot(
            jnp.where(pick, 1.0, 0.0).astype(jnp.bfloat16),
            spread.astype(jnp.bfloat16),
            preferred_element_type=jnp.float32,
        )
        return gathered[:steps].astype(jnp.bfloat16)

    def own_head(mixed):
        mixed = jnp.where(diag, mixed, 0.0)
        half = mixed[: 2 * steps]
        for g in range(1, group // 2):
            half = half + mixed[2 * steps * g : 2 * steps * (g + 1)]
        return (half[:steps] + half[steps:]).astype(jnp.bfloat16)

    def largest(x):
        return jnp.max(x, axis=1, keepdims=True)

    def summed(x):
        return jnp.sum(x, axis=1, keepdims=True)

    def weighted(weight, values):
        return [
            own_head(
                jnp.dot(
                    weight[c * rows : (c + 1) * rows],
                    values(c),
                    preferred_element_type=jnp.float32,
                )
            )
            for c in range(chunks)
        ]

    for r in range(requests):
        query = jnp.where(diag_all, tiled(q_ref[r].astype(jnp.float32) * scale, group), 0.0)
        query = query.astype(jnp.bfloat16)
        query_ref[r] = query
        keys = tiled(nk_ref[r].astype(jnp.float32), group).astype(jnp.bfloat16)
        values = tiled(nv_ref[r].astype(jnp.float32), group).astype(jnp.bfloat16)
        score = against(query, lambda c: keys[:, columns(c)])
        usable = iota(score.shape, 1) <= within(iota(score.shape, 0), steps)
        score = jnp.where(usable, score, masked_score)
        top = largest(score)
        weight = jnp.where(usable, jnp.exp(score - top), 0.0)
        fresh_ref[r, :, width:] = summary(top, summed(weight))
        mixed = weighted(weight.astype(jnp.bfloat16), lambda c: values[:, columns(c)])
        for c in range(chunks):
            fresh_ref[r, :, columns(c)] = mixed[c]

    @pl.loop(0, requests)
    def _(r):
        @pl.when(left(r) <= 0)
        def _():
            shape = (steps, LANES)
            hi, mid, low = three_parts(jnp.full(shape, masked_score, jnp.float32))
            part = over(iota(shape, 1), HEADS)
            empty = jnp.where(part == 0, hi, jnp.where(part == 1, mid, low))
            out_ref[r, :, width:] = jnp.where(part < 3, empty, 0.0).astype(jnp.bfloat16)
            out_ref[r, :, :width] = jnp.zeros((steps, width), jnp.bfloat16)

    def one(r, count):
        part = pl.ds(0, count)
        move(0, r, count).wait()
        query = query_ref[r]
        score = against(query, lambda c: kbuf[r, part, columns(c)])
        if count < block:
            usable = iota(score.shape, 1) < left(r)
            score = jnp.where(usable, score, masked_score)
        top = largest(score)
        weight = jnp.exp(score - top)
        if count < block:
            weight = jnp.where(usable, weight, 0.0)
        total = summed(weight)
        weight = weight.astype(jnp.bfloat16)
        move(1, r, count).wait()
        mixed = weighted(weight, lambda c: vbuf[r, part, columns(c)])
        out_ref[r, :, width:] = summary(top, total)
        for c in range(chunks):
            out_ref[r, :, columns(c)] = mixed[c]

    for kind, count in ((is_short, SHORT), (is_full, block)):

        @pl.loop(0, requests)
        def _(r):
            @pl.when(kind(r))
            def _():
                one(r, count)


def project(count, columns, ids_ref, hidden_ref, gain_ref, weight_ref, *refs):
    parts = refs[:count]
    attn_ref, own_ref, send_ref, attn_buf, res_buf = refs[count:]
    requests, steps, width = hidden_ref.shape
    feature = attn_ref.shape[2]
    head = width // HEADS
    seq = lax.axis_index("seq")
    tp = lax.axis_index("tp")

    def moved(x, amount):
        return pltpu.roll(x, LANES - amount, 1)

    def rows_of(ref, lanes):
        pieces = [ref[r, :, lanes].astype(jnp.float32) for r in range(requests)]
        blank = jnp.zeros((ROWS - requests * steps, pieces[0].shape[1]), jnp.float32)
        return jnp.concatenate(pieces + [blank], axis=0)

    tops, totals = [], []
    for ref in parts:
        x = rows_of(ref, slice(width, width + LANES))
        tops.append(x + moved(x, HEADS) + moved(x, 2 * HEADS))
        totals.append(moved(x, 3 * HEADS) + moved(x, 4 * HEADS) + moved(x, 5 * HEADS))
    overall = functools.reduce(jnp.maximum, tops)
    factors = [jnp.exp(top - overall) for top in tops]
    total = functools.reduce(jnp.add, [f * t for f, t in zip(factors, totals)])
    real = (iota(total.shape, 1) < HEADS) & (iota(total.shape, 0) < requests * steps)
    inverse = jnp.where(real, 1.0 / jnp.where(real, total, 1.0), 0.0)
    ratio = jnp.concatenate([jnp.where(real, f, 0.0) * inverse for f in factors], axis=0)
    expand = jnp.where(
        (within(iota((LANES, width), 0), HEADS) == over(iota((LANES, width), 1), head))
        & (iota((LANES, width), 0) < 3 * HEADS),
        1.0,
        0.0,
    ).astype(jnp.bfloat16)
    hi, mid, low = three_parts(ratio)
    packed = hi + pltpu.roll(mid, HEADS, 1) + pltpu.roll(low, 2 * HEADS, 1)
    wide = jnp.dot(packed.astype(jnp.bfloat16), expand, preferred_element_type=jnp.float32)
    context = jnp.zeros((ROWS, width), jnp.float32)
    for b, ref in enumerate(parts):
        context = context + wide[b * ROWS : (b + 1) * ROWS] * rows_of(ref, slice(0, width))
    attention = jnp.dot(
        context.astype(jnp.bfloat16), weight_ref[...], preferred_element_type=jnp.float32
    )
    residual = rows_of(hidden_ref, slice(0, width)) + attention
    normed = (
        residual
        * lax.rsqrt(jnp.mean(residual * residual, axis=1, keepdims=True) + norm_epsilon)
        * gain_ref[...]
    )
    row = iota((ROWS, columns), 0)
    lane = iota((ROWS, columns), 1) - tp * ROWS
    extra = jnp.where((lane >= 0) & (lane < ROWS), -1.0, 0.0)
    for i in range(requests * steps):
        first, second = [
            ids_ref[i // steps, k, i % steps].astype(jnp.float32) for k in range(2)
        ]
        extra = jnp.where(lane == i, jnp.where(row == requests * steps, first, second), extra)
    tail = row >= requests * steps
    message = jnp.concatenate(
        [jnp.where(tail, extra, normed[:, :columns]), normed[:, columns:]], axis=1
    ).astype(jnp.bfloat16)
    send_ref[...] = message
    attn_buf[...] = attention
    res_buf[...] = residual
    lanes = pl.ds(pl.multiple_of(seq * feature, feature), feature)
    mine = attn_buf[:, lanes]
    for r in range(requests):
        attn_ref[r] = mine[r * steps : (r + 1) * steps].astype(jnp.bfloat16)
    rest = res_buf[:, lanes]
    for r in range(requests):
        own_ref[r] = rest[r * steps : (r + 1) * steps]


def feed(
    capacity, steps, used, slices, router_ref, gate_ref, up_ref, down_ref, near_ref, far_ref,
    out_ref, tokens,
):
    half = near_ref.shape[0]
    count = 2 * half
    width = gate_ref.shape[1]
    experts = router_ref.shape[0]
    seq_size, _, requests, _, feature = out_ref.shape
    seq = lax.axis_index("seq")
    tp = lax.axis_index("tp")
    columns = count * ROWS
    core = within(tp, 2)
    for d in range(half):
        chip = over(tp, 2) ^ d
        for ref, which in ((near_ref, core), (far_ref, 1 - core)):
            start = pl.multiple_of((2 * chip + which) * ROWS, ROWS)
            tokens[pl.ds(start, ROWS), :] = ref[d]
    ids = jnp.zeros((8, columns), jnp.float32)
    for p in range(count):
        ids = ids + tokens[p * ROWS : (p + 1) * ROWS, :columns].astype(jnp.float32)[8:]
    place = used - 8
    first = ids[place : place + 1]
    second = ids[place + 1 : place + 2]
    mine = over(seq * count + tp, slices)
    mine_f = mine.astype(jnp.float32)
    hit = jnp.where((first == mine_f) | (second == mine_f), 1.0, 0.0)
    other = jnp.where(first == mine_f, second, first)
    earlier = (iota((columns, columns), 0) < iota((columns, columns), 1)) & (
        within(iota((columns, columns), 0), steps) == within(iota((columns, columns), 1), steps)
    )
    slot = jnp.dot(
        jnp.broadcast_to(hit, (ROWS, columns)).astype(jnp.bfloat16),
        jnp.where(earlier, 1.0, 0.0).astype(jnp.bfloat16),
        preferred_element_type=jnp.float32,
    )[:1]
    rows = -(-steps * capacity // ROWS) * ROWS
    row = iota((rows, columns), 0)
    choose = (
        (hit > 0.5)
        & (slot == within(row, capacity).astype(jnp.float32))
        & (within(iota((rows, columns), 1), steps) == over(row, capacity))
    )
    select = jnp.where(choose, 1.0, 0.0)
    rival = jnp.sum(select * other, axis=1, keepdims=True)
    select = select.astype(jnp.bfloat16)
    buffer = jnp.dot(select, tokens[...], preferred_element_type=jnp.float32).astype(jnp.bfloat16)
    logits = lax.dot_general(buffer, router_ref[...], NT, preferred_element_type=jnp.float32)
    index = iota((rows, experts), 1)
    ahead = jnp.sum(jnp.where(index == mine, logits, 0.0), axis=1, keepdims=True)
    behind = jnp.sum(
        jnp.where(index.astype(jnp.float32) == rival, logits, 0.0), axis=1, keepdims=True
    )
    share = 1.0 / (1.0 + jnp.exp(behind - ahead))
    gate = lax.dot_general(buffer, gate_ref[...], NT, preferred_element_type=jnp.float32)
    upward = lax.dot_general(buffer, up_ref[...], NT, preferred_element_type=jnp.float32)
    inner = (jax.nn.gelu(gate) * upward).astype(jnp.bfloat16)
    produced = jnp.dot(inner, down_ref[...], preferred_element_type=jnp.float32)
    shared = (produced * share).astype(jnp.bfloat16)
    term = lax.dot_general(select, shared, TN, preferred_element_type=jnp.float32)
    for s in range(seq_size):
        for p in range(count):
            for r in range(requests):
                start = p * ROWS + r * steps
                out_ref[s, p, r] = term[
                    start : start + steps, s * feature : (s + 1) * feature
                ].astype(jnp.bfloat16)


def limit(mebibytes):
    return pltpu.CompilerParams(vmem_limit_bytes=mebibytes * 1024 * 1024)


def stage(count, *refs):
    sources, copies, sems = refs[1 : 1 + count], refs[1 + count : 1 + 2 * count], refs[-1]
    moves = [
        pltpu.make_async_copy(source, copy, sems.at[i])
        for i, (source, copy) in enumerate(zip(sources, copies))
    ]
    for move in moves:
        move.start()
    for move in moves:
        move.wait()


def staged(after, *arrays, result=None):
    anywhere = pl.BlockSpec(memory_space=pl.ANY)
    inputs = [pltpu.with_memory_space_constraint(x, pltpu.HBM) for x in arrays]
    shapes = [pltpu.VMEM(x.shape, x.dtype) for x in arrays]
    if result is not None:
        inputs.append(result)
        shapes.append(pltpu.HBM(result.shape, result.dtype))
    count = len(inputs)
    size = sum(2 * x.size for x in arrays)
    return pl.pallas_call(
        functools.partial(stage, count),
        out_shape=tuple(shapes),
        in_specs=[anywhere] * (1 + count),
        out_specs=(anywhere,) * count,
        scratch_shapes=[pltpu.SemaphoreType.DMA((count,))],
        compiler_params=limit(4),
        cost_estimate=pl.CostEstimate(flops=0, bytes_accessed=2 * size, transcendentals=0),
        name="stage",
    )(after, *inputs)


def body(
    hidden_in,
    new_query,
    new_key,
    new_value,
    key_cache,
    value_cache,
    lengths,
    out_weight,
    norm_gain,
    router_weight,
    expert_ids,
    gate_weight,
    up_weight,
    down_weight,
):
    requests, steps, width = hidden_in.shape
    block = key_cache.shape[1]
    seq_size = lax.axis_size("seq")
    tp_size = lax.axis_size("tp")
    feature = width // seq_size
    experts = router_weight.shape[1]
    topk = expert_ids.shape[2]
    capacity = (5 * requests * tp_size * topk + 4 * experts - 1) // (4 * experts)
    slices = seq_size * tp_size // experts
    vmem = pl.BlockSpec(memory_space=pltpu.VMEM)
    smem = pl.BlockSpec(memory_space=pltpu.SMEM)
    hbm = pl.BlockSpec(memory_space=pltpu.HBM)

    small = pltpu.VMEM((requests, steps, width), jnp.bfloat16)
    partial = pltpu.VMEM((requests, steps, width + LANES), jnp.bfloat16)
    part, fresh = pl.pallas_call(
        attend,
        out_shape=(partial, partial),
        in_specs=[hbm] * 6,
        out_specs=(vmem, vmem),
        scratch_shapes=[
            pltpu.SMEM((requests,), jnp.int32),
            small,
            small,
            small,
            pltpu.VMEM((requests, ROWS, width), jnp.bfloat16),
            pltpu.VMEM((requests, block, width), jnp.bfloat16),
            pltpu.VMEM((requests, block, width), jnp.bfloat16),
            pltpu.SemaphoreType.DMA((2, requests)),
            pltpu.SemaphoreType.DMA((4,)),
        ],
        compiler_params=limit(24),
        name="attend",
    )(
        *[
            pltpu.with_memory_space_constraint(x, pltpu.HBM)
            for x in (lengths, new_query, new_key, new_value, key_cache, value_cache)
        ]
    )

    def swapped(x, axis, size, d):
        return lax.ppermute(x, axis, [(i, i ^ d) for i in range(size)])

    out_weight, gate_weight = staged(part, out_weight, gate_weight)
    parts = [fresh, part] + [swapped(part, "seq", seq_size, d) for d in range(1, seq_size)]
    attn_out, own_residual, packed = pl.pallas_call(
        functools.partial(project, seq_size + 1, tp_size * ROWS),
        out_shape=(
            pltpu.VMEM((requests, steps, feature), jnp.bfloat16),
            jax.ShapeDtypeStruct((requests, steps, feature), jnp.float32),
            jax.ShapeDtypeStruct((ROWS, width), jnp.bfloat16),
        ),
        in_specs=[smem] + [vmem] * (4 + seq_size),
        out_specs=(vmem, vmem, vmem),
        scratch_shapes=[
            pltpu.VMEM((ROWS, width), jnp.float32),
            pltpu.VMEM((ROWS, width), jnp.float32),
        ],
        compiler_params=limit(8),
        name="project",
    )(expert_ids.transpose(0, 2, 1), hidden_in, norm_gain.reshape(1, width), out_weight, *parts)
    up_weight, down_weight, attn_out = staged(packed, up_weight, down_weight, result=attn_out)
    near = jnp.stack(
        [packed] + [swapped(packed, "tp", tp_size, 2 * d) for d in range(1, tp_size // 2)]
    )
    near, up_weight, down_weight = lax.optimization_barrier((near, up_weight, down_weight))
    far = swapped(near, "tp", tp_size, 1)
    terms = pl.pallas_call(
        functools.partial(feed, capacity, steps, requests * steps, slices),
        out_shape=pltpu.VMEM((seq_size, tp_size, requests, steps, feature), jnp.bfloat16),
        in_specs=[vmem] * 6,
        out_specs=vmem,
        scratch_shapes=[pltpu.VMEM((tp_size * ROWS, width), jnp.bfloat16)],
        compiler_params=limit(16),
        name="feed",
    )(router_weight.T, gate_weight, up_weight, down_weight, near, far)
    terms = terms.reshape(seq_size * tp_size, requests, steps, feature)
    arrived = lax.all_to_all(terms, ("seq", "tp"), 0, 0, tiled=True)
    mixture = jnp.sum(arrived.astype(jnp.float32), axis=0)
    return (attn_out, (own_residual + mixture).astype(jnp.bfloat16))


def solution(mesh):
    return jax.shard_map(
        body,
        mesh=mesh,
        in_specs=(
            P("tp", None, None),
            P("tp", None, None),
            P("tp", None, None),
            P("tp", None, None),
            P("tp", "seq", None),
            P("tp", "seq", None),
            P("tp"),
            P(),
            P(),
            P(),
            P("tp", None, None),
            P(("seq", "tp"), None),
            P(("seq", "tp"), None),
            P(("seq", "tp"), None),
        ),
        out_specs=(P("tp", None, "seq"), P("tp", None, "seq")),
        check_vma=False,
    )
```

profile of v0, /device:TPU:1, one launch (start us, length us, event | category | flops | bytes accessed | tf_op | source)
XLA Modules:
  0.0 39.7 jit_solution(11619981200864410089)
XLA Ops:
  0.6 5.0 %attend.1 = (bf16[3,4,1152]{2,1,0:T(4,128)(2,1)S(1)}, bf16[3,4,1152]{2,1,0:T(4,128)(2,1)S(1)}) custom-call(s32[3]{0:T(128)} %lens_hbm.1, bf16[3,4,1024]{2,1,0:T(4,128)(2,1)} %q_hbm.1, bf16[3,4,1024]{2,1,0:T(4,128)(2,1)} %nk_hbm.1, bf16[3,4,1024]{2,1,0:T(4,128)(2,1)} %nv_hbm.1, bf16[3,1024,1024]{2,1,0:T(8,128)(2,1)} %k_hbm.1, bf16[3,1024,1024]{2,1,0:T(8,128)(2,1)} %v_hbm.1), custom_call_target="tpu_custom_call" | custom-call | tf_op jit(solution)/shard_map/attend/pallas_call | solution.py:418
  5.7 0.0 copy-start.1
  5.7 0.0 copy-start.2
  5.7 0.0 copy-start.3
  5.7 2.9 %collective-permute-start.2 = (bf16[3,4,1152]{2,1,0:T(4,128)(2,1)S(1)}, bf16[3,4,1152]{2,1,0:T(4,128)(2,1)S(1)}, u32[]{:S(2)}, u32[]{:S(2)}) collective-permute-start(bf16[3,4,1152]{2,1,0:T(4,128)(2,1)S(1)} %get-tuple-element.15.refs_0_.refs_1_), channel_id=1, source_target_pairs={{0,24},{8,16},{16,8},{24,0},{1,25},{9,17},{17,9},{25,1},{2,26},{10... | collective-permute-start | bytes 82952 | tf_op jit(solution)/shard_map/ppermute | solution.py:444
  8.6 0.2 collective-permute-start.1
  8.8 0.1 collective-permute-start
  9.0 2.5 %stage.2 = (bf16[1024,1024]{1,0:T(8,128)(2,1)S(1)}, bf16[1408,1024]{1,0:T(8,128)(2,1)S(1)}) custom-call(bf16[3,4,1152]{2,1,0:T(4,128)(2,1)S(1)} %get-tuple-element.15.refs_0_.refs_1_, bf16[1024,1024]{1,0:T(8,128)(2,1)} %refs_1_.2, bf16[1408,1024]{1,0:T(8,128)(2,1)} %refs_2_.2), custom_call_target="tpu_custom_call" | custom-call | bytes 9961472 | tf_op jit(solution)/shard_map/stage/pallas_call | solution.py:375
  11.4 0.0 collective-permute-done.2.refs_4_
  11.4 0.3 collective-permute-done.1.refs_3_
  11.7 0.1 collective-permute-done.refs_2_
  11.8 0.0 copy-done.1
  11.8 0.0 copy-done.2
  11.8 0.0 copy-done.3
  11.8 1.4 %project.1 = (bf16[3,4,256]{2,1,0:T(4,128)(2,1)S(1)}, f32[3,4,256]{2,1,0:T(4,128)S(1)}, bf16[16,1024]{1,0:T(8,128)(2,1)S(1)}) custom-call(s32[3,2,4]{2,1,0:T(2,128)S(1)} %bitcast.12, bf16[3,4,1024]{2,1,0:T(4,128)(2,1)S(1)} %copy-done.1, f32[1,1024]{1,0:T(1,128)S(1)} %bitcast.11, bf16[1024,1024]{1,0:T(8,128)(2,1)S(1)} %get-tuple-element.16.weight_ref, ...), custom_call_target="tpu_custom_call" | custom-call | tf_op jit(solution)/shard_map/project/pallas_call | solution.py:448
  13.2 2.4 %collective-permute-start.5 = (bf16[16,1024]{1,0:T(8,128)(2,1)S(1)}, bf16[16,1024]{1,0:T(8,128)(2,1)S(1)}, u32[]{:S(2)}, u32[]{:S(2)}) collective-permute-start(bf16[16,1024]{1,0:T(8,128)(2,1)S(1)} %get-tuple-element.18.refs_0_), channel_id=1, source_target_pairs={{0,6},{1,7},{2,4},{3,5},{4,2},{5,3},{6,0},{7,1},{8,14},{9,15},{10,... | collective-permute-start | bytes 98312 | tf_op jit(solution)/shard_map/ppermute | solution.py:444
  15.7 0.0 collective-permute-start.4
  15.7 1.2 %collective-permute-start.3 = (bf16[16,1024]{1,0:T(8,128)(2,1)S(1)}, bf16[16,1024]{1,0:T(8,128)(2,1)S(1)}, u32[]{:S(2)}, u32[]{:S(2)}) collective-permute-start(bf16[16,1024]{1,0:T(8,128)(2,1)S(1)} %get-tuple-element.18.refs_0_), channel_id=1, source_target_pairs={{0,2},{1,3},{2,0},{3,1},{4,6},{5,7},{6,4},{7,5},{8,10},{9,11},{10,... | collective-permute-start | bytes 98312 | tf_op jit(solution)/shard_map/ppermute | solution.py:444
  16.8 0.0 copy-start
  16.8 2.7 %stage.3 = (bf16[1408,1024]{1,0:T(8,128)(2,1)S(1)}, bf16[1408,1024]{1,0:T(8,128)(2,1)S(1)}, bf16[3,4,256]{2,1,0:T(4,128)(2,1)}) custom-call(bf16[16,1024]{1,0:T(8,128)(2,1)S(1)} %get-tuple-element.18.refs_0_, bf16[1408,1024]{1,0:T(8,128)(2,1)} %refs_1_.3, bf16[1408,1024]{1,0:T(8,128)(2,1)} %refs_2_.3, bf16[3,4,256]{2,1,0:T(4,128)(2,1)S(1)} %get-tuple-element.19.refs_3_), custom_call_target="tpu_custom_call" | custom-call | bytes 11534336 | tf_op jit(solution)/shard_map/stage/pallas_call | solution.py:375
  19.6 0.0 collective-permute-done.5
  19.6 0.0 collective-permute-done.4
  19.6 0.0 collective-permute-done.3
  19.6 3.0 %collective-permute-start.6 = (bf16[4,16,1024]{2,1,0:T(8,128)(2,1)S(1)}, bf16[4,16,1024]{2,1,0:T(8,128)(2,1)S(1)}, u32[]{:S(2)}, u32[]{:S(2)}) collective-permute-start(bf16[4,16,1024]{2,1,0:T(8,128)(2,1)S(1)} %pad_maximum_fusion.near_ref), channel_id=1, source_target_pairs={{0,1},{1,0},{2,3},{3,2},{4,5},{5,4},{6,7},{7,6},{8,9},{9,8},{10,11... | collective-permute-start | bytes 393224 | tf_op jit(solution)/shard_map/ppermute | solution.py:444
  22.6 1.0 %collective-permute-done.6.far_ref = bf16[4,16,1024]{2,1,0:T(8,128)(2,1)S(1)} collective-permute-done((bf16[4,16,1024]{2,1,0:T(8,128)(2,1)S(1)}, bf16[4,16,1024]{2,1,0:T(8,128)(2,1)S(1)}, u32[]{:S(2)}, u32[]{:S(2)}) %collective-permute-start.6) | collective-permute-done | bytes 131104 | tf_op jit(solution)/shard_map/ppermute | solution.py:444
  23.6 0.0 copy-done
  23.6 2.4 %feed.1 = bf16[4,8,3,4,256]{4,3,2,1,0:T(4,128)(2,1)S(1)} custom-call(bf16[16,1024]{1,0:T(8,128)(2,1)S(1)} %bitcast.10, bf16[1408,1024]{1,0:T(8,128)(2,1)S(1)} %get-tuple-element.22.gate_ref, bf16[1408,1024]{1,0:T(8,128)(2,1)S(1)} %get-tuple-element.25.up_ref, bf16[1408,1024]{1,0:T(8,128)(2,1)S(1)} %get-tuple-element.26.down_ref, ...), custom_call_target="tpu_custom_call" | custom-call | tf_op jit(solution)/shard_map/feed/pallas_call | solution.py:470
  26.0 13.0 %all_to_all.5 = bf16[32,3,4,256]{3,2,1,0:T(4,128)(2,1)S(1)} all-to-all(bf16[32,3,4,256]{3,2,1,0:T(4,128)(2,1)S(1)} %bitcast.8), channel_id=1, replica_groups=mesh['seq'=4,'tp'=8] {'seq','tp'}, dimensions={0} | all-to-all | bytes 393216 | tf_op jit(solution)/shard_map/all_to_all | solution.py:480
  39.0 0.1 convert_reduce_fusion
  39.1 0.6 %add_convert_fusion = bf16[3,4,256]{2,1,0:T(4,128)(2,1)} fusion(f32[3,4,256]{2,1,0:T(4,128)S(1)} %get-tuple-element.21, f32[3,4,256]{2,1,0:T(4,128)S(1)} %convert_reduce_fusion), kind=kLoop, calls=%fused_computation.2 | loop fusion | flops 6144 | bytes 30720 | tf_op jit(solution)/shard_map/convert_element_type | solution.py:482
  (1 shorter events, 0.0 us)
Async XLA Ops:
  5.7 6.2 %copy-start.1 = (bf16[3,4,1024]{2,1,0:T(4,128)(2,1)S(1)}, bf16[3,4,1024]{2,1,0:T(4,128)(2,1)}, u32[]{:S(2)}) copy-start(bf16[3,4,1024]{2,1,0:T(4,128)(2,1)} %hidden_ref.1) | copy-start | bytes 73732
  5.7 6.1 %copy-start.2 = (f32[1024]{0:T(1024)S(1)}, f32[1024]{0:T(1024)}, u32[]{:S(2)}) copy-start(f32[1024]{0:T(1024)} %param.22) | copy-start | bytes 12292
  5.7 6.1 %copy-start.3 = (s32[3,4,2]{1,2,0:T(2,128)S(1)}, s32[3,4,2]{1,2,0:T(2,128)}, u32[]{:S(2)}) copy-start(s32[3,4,2]{1,2,0:T(2,128)} %param.24) | copy-start | bytes 292
  5.7 5.7 %collective-permute-start.2 = (bf16[3,4,1152]{2,1,0:T(4,128)(2,1)S(1)}, bf16[3,4,1152]{2,1,0:T(4,128)(2,1)S(1)}, u32[]{:S(2)}, u32[]{:S(2)}) collective-permute-start(bf16[3,4,1152]{2,1,0:T(4,128)(2,1)S(1)} %get-tuple-element.15.refs_0_.refs_1_), channel_id=1, source_target_pairs={{0,24},{8,16},{16,8},{24,0},{1,25},{9,17},{17,9},{25,1},{2,26},{10... | collective-permute-start | bytes 82952 | tf_op jit(solution)/shard_map/ppermute | solution.py:444
  8.6 3.1 %collective-permute-start.1 = (bf16[3,4,1152]{2,1,0:T(4,128)(2,1)S(1)}, bf16[3,4,1152]{2,1,0:T(4,128)(2,1)S(1)}, u32[]{:S(2)}, u32[]{:S(2)}) collective-permute-start(bf16[3,4,1152]{2,1,0:T(4,128)(2,1)S(1)} %get-tuple-element.15.refs_0_.refs_1_), channel_id=1, source_target_pairs={{0,16},{8,24},{16,0},{24,8},{1,17},{9,25},{17,1},{25,9},{2,18},{10... | collective-permute-start | bytes 82952 | tf_op jit(solution)/shard_map/ppermute | solution.py:444
  8.8 3.0 %collective-permute-start = (bf16[3,4,1152]{2,1,0:T(4,128)(2,1)S(1)}, bf16[3,4,1152]{2,1,0:T(4,128)(2,1)S(1)}, u32[]{:S(2)}, u32[]{:S(2)}) collective-permute-start(bf16[3,4,1152]{2,1,0:T(4,128)(2,1)S(1)} %get-tuple-element.15.refs_0_.refs_1_), channel_id=1, source_target_pairs={{0,8},{8,0},{16,24},{24,16},{1,9},{9,1},{17,25},{25,17},{2,10},{10... | collective-permute-start | bytes 82952 | tf_op jit(solution)/shard_map/ppermute | solution.py:444
  13.2 6.3 %collective-permute-start.5 = (bf16[16,1024]{1,0:T(8,128)(2,1)S(1)}, bf16[16,1024]{1,0:T(8,128)(2,1)S(1)}, u32[]{:S(2)}, u32[]{:S(2)}) collective-permute-start(bf16[16,1024]{1,0:T(8,128)(2,1)S(1)} %get-tuple-element.18.refs_0_), channel_id=1, source_target_pairs={{0,6},{1,7},{2,4},{3,5},{4,2},{5,3},{6,0},{7,1},{8,14},{9,15},{10,... | collective-permute-start | bytes 98312 | tf_op jit(solution)/shard_map/ppermute | solution.py:444
  15.7 3.9 %collective-permute-start.4 = (bf16[16,1024]{1,0:T(8,128)(2,1)S(1)}, bf16[16,1024]{1,0:T(8,128)(2,1)S(1)}, u32[]{:S(2)}, u32[]{:S(2)}) collective-permute-start(bf16[16,1024]{1,0:T(8,128)(2,1)S(1)} %get-tuple-element.18.refs_0_), channel_id=1, source_target_pairs={{0,4},{1,5},{2,6},{3,7},{4,0},{5,1},{6,2},{7,3},{8,12},{9,13},{10,... | collective-permute-start | bytes 98312 | tf_op jit(solution)/shard_map/ppermute | solution.py:444
  15.7 3.9 %collective-permute-start.3 = (bf16[16,1024]{1,0:T(8,128)(2,1)S(1)}, bf16[16,1024]{1,0:T(8,128)(2,1)S(1)}, u32[]{:S(2)}, u32[]{:S(2)}) collective-permute-start(bf16[16,1024]{1,0:T(8,128)(2,1)S(1)} %get-tuple-element.18.refs_0_), channel_id=1, source_target_pairs={{0,2},{1,3},{2,0},{3,1},{4,6},{5,7},{6,4},{7,5},{8,10},{9,11},{10,... | collective-permute-start | bytes 98312 | tf_op jit(solution)/shard_map/ppermute | solution.py:444
  16.8 6.8 %copy-start = (bf16[1024,16]{0,1:T(8,128)(2,1)S(1)}, bf16[1024,16]{0,1:T(8,128)(2,1)}, u32[]{:S(2)}) copy-start(bf16[1024,16]{0,1:T(8,128)(2,1)} %param.23) | copy-start | bytes 98308
  19.6 4.0 %collective-permute-start.6 = (bf16[4,16,1024]{2,1,0:T(8,128)(2,1)S(1)}, bf16[4,16,1024]{2,1,0:T(8,128)(2,1)S(1)}, u32[]{:S(2)}, u32[]{:S(2)}) collective-permute-start(bf16[4,16,1024]{2,1,0:T(8,128)(2,1)S(1)} %pad_maximum_fusion.near_ref), channel_id=1, source_target_pairs={{0,1},{1,0},{2,3},{3,2},{4,5},{5,4},{6,7},{7,6},{8,9},{9,8},{10,11... | collective-permute-start | bytes 393224 | tf_op jit(solution)/shard_map/ppermute | solution.py:444
where the time goes:
time: 39.3 us; the launch traced here: 39.7 us
  Pallas kernels  14 us (36%)
  blocking collectives  13 us (33%)
  starting transfers between devices  9.85 us (25%)
  waiting for transfers between devices  1.38 us (4%)
  between operations  0.74 us (2%)
  other arithmetic  0.72 us (2%)
    all_to_all x1, blocking collectives, body(): arrived = lax.all_to_all(terms, ('seq', 'tp'), 0, 0, tiled=True)  13 us
    ppermute x7, starting transfers between devices, swapped(): return lax.ppermute(x, axis, [(i, i ^ d) for i in range(size)])  9.85 us
    pallas_call x2, Pallas kernels, staged(): pl.pallas_call(functools.partial(stage, count), out_shape=tuple(shapes),...  5.18 us
    pallas_call x1, Pallas kernels, body(): pl.pallas_call(attend, out_shape=(partial, partial), in_specs=[hbm] * 6,...  5.03 us
    pallas_call x1, Pallas kernels, body(): pl.pallas_call(functools.partial(feed, capacity, steps, requests * steps,...  2.43 us
    ppermute x7, waiting for transfers between devices, swapped(): return lax.ppermute(x, axis, [(i, i ^ d) for i in range(size)])  1.38 us
    pallas_call x1, Pallas kernels, body(): pl.pallas_call(functools.partial(project, seq_size + 1, tp_size * ROWS),...  1.37 us
  transfers between devices with their start and end apart: 7, of which 3 were waited for; matrix products, arithmetic and copies ran while one was open for 0% of the time, Pallas kernels for 13%

commit v1 on v0

--- a/solution.py
+++ b/solution.py
@@ -205,14 +205,13 @@
                 one(r, count)
 
 
-def project(count, columns, ids_ref, hidden_ref, gain_ref, weight_ref, *refs):
+def project(count, ids_ref, hidden_ref, gain_ref, weight_ref, *refs):
     parts = refs[:count]
     attn_ref, own_ref, send_ref, attn_buf, res_buf = refs[count:]
     requests, steps, width = hidden_ref.shape
     feature = attn_ref.shape[2]
     head = width // HEADS
     seq = lax.axis_index("seq")
-    tp = lax.axis_index("tp")
 
     def moved(x, amount):
         return pltpu.roll(x, LANES - amount, 1)
@@ -234,14 +233,15 @@
     inverse = jnp.where(real, 1.0 / jnp.where(real, total, 1.0), 0.0)
     ratio = jnp.concatenate([jnp.where(real, f, 0.0) * inverse for f in factors], axis=0)
     expand = jnp.where(
-        (within(iota((LANES, width), 0), HEADS) == over(iota((LANES, width), 1), head))
-        & (iota((LANES, width), 0) < 3 * HEADS),
+        (within(iota((4 * HEADS, width), 0), HEADS) == over(iota((4 * HEADS, width), 1), head))
+        & (iota((4 * HEADS, width), 0) < 3 * HEADS),
         1.0,
         0.0,
     ).astype(jnp.bfloat16)
     hi, mid, low = three_parts(ratio)
     packed = hi + pltpu.roll(mid, HEADS, 1) + pltpu.roll(low, 2 * HEADS, 1)
-    wide = jnp.dot(packed.astype(jnp.bfloat16), expand, preferred_element_type=jnp.float32)
+    packed = packed.astype(jnp.bfloat16)[:, : 4 * HEADS]
+    wide = jnp.dot(packed, expand, preferred_element_type=jnp.float32)
     context = jnp.zeros((ROWS, width), jnp.float32)
     for b, ref in enumerate(parts):
         context = context + wide[b * ROWS : (b + 1) * ROWS] * rows_of(ref, slice(0, width))
@@ -254,19 +254,17 @@
         * lax.rsqrt(jnp.mean(residual * residual, axis=1, keepdims=True) + norm_epsilon)
         * gain_ref[...]
     )
-    row = iota((ROWS, columns), 0)
-    lane = iota((ROWS, columns), 1) - tp * ROWS
-    extra = jnp.where((lane >= 0) & (lane < ROWS), -1.0, 0.0)
+    row = iota((ROWS, LANES), 0)
+    lane = iota((ROWS, LANES), 1)
+    extra = jnp.zeros((ROWS, LANES), jnp.float32)
     for i in range(requests * steps):
-        first, second = [
-            ids_ref[i // steps, k, i % steps].astype(jnp.float32) for k in range(2)
-        ]
-        extra = jnp.where(lane == i, jnp.where(row == requests * steps, first, second), extra)
-    tail = row >= requests * steps
-    message = jnp.concatenate(
-        [jnp.where(tail, extra, normed[:, :columns]), normed[:, columns:]], axis=1
-    ).astype(jnp.bfloat16)
-    send_ref[...] = message
+        for k in range(2):
+            number = ids_ref[i // steps, k, i % steps].astype(jnp.float32)
+            extra = jnp.where((row == i) & (lane == k), number, extra)
+    for r in range(requests):
+        part = slice(r * steps, (r + 1) * steps)
+        send_ref[r, :, :width] = normed[part].astype(jnp.bfloat16)
+        send_ref[r, :, width:] = extra[part].astype(jnp.bfloat16)
     attn_buf[...] = attention
     res_buf[...] = residual
     lanes = pl.ds(pl.multiple_of(seq * feature, feature), feature)
@@ -295,16 +293,23 @@
         chip = over(tp, 2) ^ d
         for ref, which in ((near_ref, core), (far_ref, 1 - core)):
             start = pl.multiple_of((2 * chip + which) * ROWS, ROWS)
-            tokens[pl.ds(start, ROWS), :] = ref[d]
-    ids = jnp.zeros((8, columns), jnp.float32)
-    for p in range(count):
-        ids = ids + tokens[p * ROWS : (p + 1) * ROWS, :columns].astype(jnp.float32)[8:]
-    place = used - 8
-    first = ids[place : place + 1]
-    second = ids[place + 1 : place + 2]
+            pieces = [ref[d, r].astype(jnp.float32) for r in range(requests)]
+            blank = jnp.zeros((ROWS - used, pieces[0].shape[1]), jnp.float32)
+            rows_of = jnp.concatenate(pieces + [blank], axis=0)
+            tokens[pl.ds(start, ROWS), :] = rows_of.astype(jnp.bfloat16)
+    turn = iota((ROWS, LANES), 0) == iota((ROWS, LANES), 1)
+    ids = lax.dot_general(
+        jnp.where(turn, 1.0, 0.0).astype(jnp.bfloat16),
+        tokens[:, width:],
+        NT,
+        preferred_element_type=jnp.float32,
+    )
+    first = ids[:1]
+    second = ids[1:2]
+    real = within(iota((1, columns), 1), ROWS) < used
     mine = over(seq * count + tp, slices)
     mine_f = mine.astype(jnp.float32)
-    hit = jnp.where((first == mine_f) | (second == mine_f), 1.0, 0.0)
+    hit = jnp.where(((first == mine_f) | (second == mine_f)) & real, 1.0, 0.0)
     other = jnp.where(first == mine_f, second, first)
     earlier = (iota((columns, columns), 0) < iota((columns, columns), 1)) & (
         within(iota((columns, columns), 0), steps) == within(iota((columns, columns), 1), steps)
@@ -324,7 +329,7 @@
     select = jnp.where(choose, 1.0, 0.0)
     rival = jnp.sum(select * other, axis=1, keepdims=True)
     select = select.astype(jnp.bfloat16)
-    buffer = jnp.dot(select, tokens[...], preferred_element_type=jnp.float32).astype(jnp.bfloat16)
+    buffer = jnp.dot(select, tokens[:, :width], preferred_element_type=jnp.float32).astype(jnp.bfloat16)
     logits = lax.dot_general(buffer, router_ref[...], NT, preferred_element_type=jnp.float32)
     index = iota((rows, experts), 1)
     ahead = jnp.sum(jnp.where(index == mine, logits, 0.0), axis=1, keepdims=True)
@@ -446,11 +451,11 @@
     out_weight, gate_weight = staged(part, out_weight, gate_weight)
     parts = [fresh, part] + [swapped(part, "seq", seq_size, d) for d in range(1, seq_size)]
     attn_out, own_residual, packed = pl.pallas_call(
-        functools.partial(project, seq_size + 1, tp_size * ROWS),
+        functools.partial(project, seq_size + 1),
         out_shape=(
             pltpu.VMEM((requests, steps, feature), jnp.bfloat16),
             jax.ShapeDtypeStruct((requests, steps, feature), jnp.float32),
-            jax.ShapeDtypeStruct((ROWS, width), jnp.bfloat16),
+            partial,
         ),
         in_specs=[smem] + [vmem] * (4 + seq_size),
         out_specs=(vmem, vmem, vmem),
@@ -472,7 +477,7 @@
         out_shape=pltpu.VMEM((seq_size, tp_size, requests, steps, feature), jnp.bfloat16),
         in_specs=[vmem] * 6,
         out_specs=vmem,
-        scratch_shapes=[pltpu.VMEM((tp_size * ROWS, width), jnp.bfloat16)],
+        scratch_shapes=[pltpu.VMEM((tp_size * ROWS, width + LANES), jnp.bfloat16)],
         compiler_params=limit(16),
         name="feed",
     )(router_weight.T, gate_weight, up_weight, down_weight, near, far)

time: 39.3 us -> 40.2 us (1.023); the launches traced: 39.7 us -> 40 us
  Pallas kernels: 14 us -> 12.6 us
  starting transfers between devices: 9.85 us -> 10.9 us
  waiting for transfers between devices: 1.38 us -> 1.88 us
    pallas_call x1, Pallas kernels: 5.03 us -> 3.44 us  [body(): pl.pallas_call(attend, out_shape=(partial, partial), in_specs=[hbm] * 6,...]
    ppermute x7, starting transfers between devices: 9.85 us -> 10.9 us  [swapped(): return lax.ppermute(x, axis, [(i, i ^ d) for i in range(size)])]
    ppermute x7, waiting for transfers between devices: 1.38 us -> 1.88 us  [swapped(): return lax.ppermute(x, axis, [(i, i ^ d) for i in range(size)])]
  transfers between devices with their start and end apart: 7 -> 7, of which waited for: 3 -> 2; matrix products, arithmetic and copies ran while one was open for 0% -> 0% of each run, Pallas kernels for 13% -> 13%
where the time goes in v1:
time: 40.2 us; the launch traced here: 40 us
  blocking collectives  13 us (32%)
  Pallas kernels  12.6 us (31%)
  starting transfers between devices  10.9 us (27%)
  waiting for transfers between devices  1.88 us (5%)
  other arithmetic  0.79 us (2%)
  between operations  0.76 us (2%)
    all_to_all x1, blocking collectives, body(): arrived = lax.all_to_all(terms, ('seq', 'tp'), 0, 0, tiled=True)  13 us
    ppermute x7, starting transfers between devices, swapped(): return lax.ppermute(x, axis, [(i, i ^ d) for i in range(size)])  10.9 us
    pallas_call x2, Pallas kernels, staged(): pl.pallas_call(functools.partial(stage, count), out_shape=tuple(shapes),...  5.18 us
    pallas_call x1, Pallas kernels, body(): pl.pallas_call(attend, out_shape=(partial, partial), in_specs=[hbm] * 6,...  3.44 us
    pallas_call x1, Pallas kernels, body(): pl.pallas_call(functools.partial(feed, capacity, steps, requests * steps,...  2.6 us
    ppermute x7, waiting for transfers between devices, swapped(): return lax.ppermute(x, axis, [(i, i ^ d) for i in range(size)])  1.88 us
    pallas_call x1, Pallas kernels, body(): pl.pallas_call(functools.partial(project, seq_size + 1), out_shape=(pltpu...  1.37 us
  transfers between devices with their start and end apart: 7, of which 2 were waited for; matrix products, arithmetic and copies ran while one was open for 0% of the time, Pallas kernels for 13%

profile of v1, /device:TPU:1, one launch (start us, length us, event | category | flops | bytes accessed | tf_op | source)
XLA Modules:
  0.0 40.0 jit_solution(11251313914427527782)
XLA Ops:
  0.6 3.4 %attend.1 = (bf16[3,4,1152]{2,1,0:T(4,128)(2,1)S(1)}, bf16[3,4,1152]{2,1,0:T(4,128)(2,1)S(1)}) custom-call(s32[3]{0:T(128)} %lens_hbm.1, bf16[3,4,1024]{2,1,0:T(4,128)(2,1)} %q_hbm.1, bf16[3,4,1024]{2,1,0:T(4,128)(2,1)} %nk_hbm.1, bf16[3,4,1024]{2,1,0:T(4,128)(2,1)} %nv_hbm.1, bf16[3,1024,1024]{2,1,0:T(8,128)(2,1)} %k_hbm.1, bf16[3,1024,1024]{2,1,0:T(8,128)(2,1)} %v_hbm.1), custom_call_target="tpu_custom_call" | custom-call | tf_op jit(solution)/shard_map/attend/pallas_call | solution.py:423
  4.1 0.0 copy-start.1
  4.1 0.0 copy-start.2
  4.1 0.0 copy-start.3
  4.1 1.6 %collective-permute-start.2 = (bf16[3,4,1152]{2,1,0:T(4,128)(2,1)S(1)}, bf16[3,4,1152]{2,1,0:T(4,128)(2,1)S(1)}, u32[]{:S(2)}, u32[]{:S(2)}) collective-permute-start(bf16[3,4,1152]{2,1,0:T(4,128)(2,1)S(1)} %get-tuple-element.15.refs_0_.refs_1_), channel_id=1, source_target_pairs={{0,24},{8,16},{16,8},{24,0},{1,25},{9,17},{17,9},{25,1},{2,26},{10... | collective-permute-start | bytes 82952 | tf_op jit(solution)/shard_map/ppermute | solution.py:449
  5.8 0.2 collective-permute-start.1
  6.0 0.8 %collective-permute-start = (bf16[3,4,1152]{2,1,0:T(4,128)(2,1)S(1)}, bf16[3,4,1152]{2,1,0:T(4,128)(2,1)S(1)}, u32[]{:S(2)}, u32[]{:S(2)}) collective-permute-start(bf16[3,4,1152]{2,1,0:T(4,128)(2,1)S(1)} %get-tuple-element.15.refs_0_.refs_1_), channel_id=1, source_target_pairs={{0,8},{8,0},{16,24},{24,16},{1,9},{9,1},{17,25},{25,17},{2,10},{10... | collective-permute-start | bytes 82952 | tf_op jit(solution)/shard_map/ppermute | solution.py:449
  6.8 2.5 %stage.2 = (bf16[1024,1024]{1,0:T(8,128)(2,1)S(1)}, bf16[1408,1024]{1,0:T(8,128)(2,1)S(1)}) custom-call(bf16[3,4,1152]{2,1,0:T(4,128)(2,1)S(1)} %get-tuple-element.15.refs_0_.refs_1_, bf16[1024,1024]{1,0:T(8,128)(2,1)} %refs_1_.2, bf16[1408,1024]{1,0:T(8,128)(2,1)} %refs_2_.2), custom_call_target="tpu_custom_call" | custom-call | bytes 9961472 | tf_op jit(solution)/shard_map/stage/pallas_call | solution.py:380
  9.3 0.0 collective-permute-done.2.refs_4_
  9.3 0.0 collective-permute-done.1.refs_3_
  9.3 0.0 collective-permute-done.refs_2_
  9.3 0.0 copy-done.1
  9.3 0.0 copy-done.2
  9.3 0.0 copy-done.3
  9.4 1.4 %project.1 = (bf16[3,4,256]{2,1,0:T(4,128)(2,1)S(1)}, f32[3,4,256]{2,1,0:T(4,128)S(1)}, bf16[3,4,1152]{2,1,0:T(4,128)(2,1)S(1)}) custom-call(s32[3,2,4]{2,1,0:T(2,128)S(1)} %bitcast.12, bf16[3,4,1024]{2,1,0:T(4,128)(2,1)S(1)} %copy-done.1, f32[1,1024]{1,0:T(1,128)S(1)} %bitcast.11, bf16[1024,1024]{1,0:T(8,128)(2,1)S(1)} %get-tuple-element.16.weight_ref, ...), custom_call_target="tpu_custom_call" | custom-call | tf_op jit(solution)/shard_map/project/pallas_call | solution.py:453
  10.7 4.9 %collective-permute-start.5 = (bf16[3,4,1152]{2,1,0:T(4,128)(2,1)S(1)}, bf16[3,4,1152]{2,1,0:T(4,128)(2,1)S(1)}, u32[]{:S(2)}, u32[]{:S(2)}) collective-permute-start(bf16[3,4,1152]{2,1,0:T(4,128)(2,1)S(1)} %get-tuple-element.18.refs_0_), channel_id=1, source_target_pairs={{0,6},{1,7},{2,4},{3,5},{4,2},{5,3},{6,0},{7,1},{8,14},{9,15},{10,... | collective-permute-start | bytes 82952 | tf_op jit(solution)/shard_map/ppermute | solution.py:449
  15.7 0.0 collective-permute-start.4
  15.7 0.4 collective-permute-start.3
  16.0 0.0 copy-start
  16.0 2.7 %stage.3 = (bf16[1408,1024]{1,0:T(8,128)(2,1)S(1)}, bf16[1408,1024]{1,0:T(8,128)(2,1)S(1)}, bf16[3,4,256]{2,1,0:T(4,128)(2,1)}) custom-call(bf16[3,4,1152]{2,1,0:T(4,128)(2,1)S(1)} %get-tuple-element.18.refs_0_, bf16[1408,1024]{1,0:T(8,128)(2,1)} %refs_1_.3, bf16[1408,1024]{1,0:T(8,128)(2,1)} %refs_2_.3, bf16[3,4,256]{2,1,0:T(4,128)(2,1)S(1)} %get-tuple-element.19.refs_3_), custom_call_target="tpu_custom_call" | custom-call | bytes 11534336 | tf_op jit(solution)/shard_map/stage/pallas_call | solution.py:380
  18.8 0.0 collective-permute-done.5
  18.8 0.9 %collective-permute-done.4 = bf16[3,4,1152]{2,1,0:T(4,128)(2,1)S(1)} collective-permute-done((bf16[3,4,1152]{2,1,0:T(4,128)(2,1)S(1)}, bf16[3,4,1152]{2,1,0:T(4,128)(2,1)S(1)}, u32[]{:S(2)}, u32[]{:S(2)}) %collective-permute-start.4) | collective-permute-done | bytes 27680 | tf_op jit(solution)/shard_map/ppermute | solution.py:449
  19.7 0.0 collective-permute-done.3
  19.7 0.1 pad_maximum_fusion.near_ref
  19.8 2.9 %collective-permute-start.6 = (bf16[4,3,4,1152]{3,2,1,0:T(4,128)(2,1)S(1)}, bf16[4,3,4,1152]{3,2,1,0:T(4,128)(2,1)S(1)}, u32[]{:S(2)}, u32[]{:S(2)}) collective-permute-start(bf16[4,3,4,1152]{3,2,1,0:T(4,128)(2,1)S(1)} %pad_maximum_fusion.near_ref), channel_id=1, source_target_pairs={{0,1},{1,0},{2,3},{3,2},{4,5},{5,4},{6,7},{7,6},{8,9},{9,8},{10,11... | collective-permute-start | bytes 331784 | tf_op jit(solution)/shard_map/ppermute | solution.py:449
  22.7 1.0 %collective-permute-done.6.far_ref = bf16[4,3,4,1152]{3,2,1,0:T(4,128)(2,1)S(1)} collective-permute-done((bf16[4,3,4,1152]{3,2,1,0:T(4,128)(2,1)S(1)}, bf16[4,3,4,1152]{3,2,1,0:T(4,128)(2,1)S(1)}, u32[]{:S(2)}, u32[]{:S(2)}) %collective-permute-start.6) | collective-permute-done | bytes 110624 | tf_op jit(solution)/shard_map/ppermute | solution.py:449
  23.6 0.0 copy-done
  23.6 2.6 %feed.1 = bf16[4,8,3,4,256]{4,3,2,1,0:T(4,128)(2,1)S(1)} custom-call(bf16[16,1024]{1,0:T(8,128)(2,1)S(1)} %bitcast.10, bf16[1408,1024]{1,0:T(8,128)(2,1)S(1)} %get-tuple-element.22.gate_ref, bf16[1408,1024]{1,0:T(8,128)(2,1)S(1)} %get-tuple-element.25.up_ref, bf16[1408,1024]{1,0:T(8,128)(2,1)S(1)} %get-tuple-element.26.down_ref, ...), custom_call_target="tpu_custom_call" | custom-call | tf_op jit(solution)/shard_map/feed/pallas_call | solution.py:475
  26.2 13.0 %all_to_all.5 = bf16[32,3,4,256]{3,2,1,0:T(4,128)(2,1)S(1)} all-to-all(bf16[32,3,4,256]{3,2,1,0:T(4,128)(2,1)S(1)} %bitcast.8), channel_id=1, replica_groups=mesh['seq'=4,'tp'=8] {'seq','tp'}, dimensions={0} | all-to-all | bytes 393216 | tf_op jit(solution)/shard_map/all_to_all | solution.py:485
  39.3 0.1 convert_reduce_fusion
  39.4 0.6 %add_convert_fusion = bf16[3,4,256]{2,1,0:T(4,128)(2,1)} fusion(f32[3,4,256]{2,1,0:T(4,128)S(1)} %get-tuple-element.21, f32[3,4,256]{2,1,0:T(4,128)S(1)} %convert_reduce_fusion), kind=kLoop, calls=%fused_computation.2 | loop fusion | flops 6144 | bytes 30720 | tf_op jit(solution)/shard_map/convert_element_type | solution.py:487
Async XLA Ops:
  4.1 5.3 %copy-start.1 = (bf16[3,4,1024]{2,1,0:T(4,128)(2,1)S(1)}, bf16[3,4,1024]{2,1,0:T(4,128)(2,1)}, u32[]{:S(2)}) copy-start(bf16[3,4,1024]{2,1,0:T(4,128)(2,1)} %hidden_ref.1) | copy-start | bytes 73732
  4.1 5.3 %copy-start.2 = (f32[1024]{0:T(1024)S(1)}, f32[1024]{0:T(1024)}, u32[]{:S(2)}) copy-start(f32[1024]{0:T(1024)} %param.22) | copy-start | bytes 12292
  4.1 5.3 %copy-start.3 = (s32[3,4,2]{1,2,0:T(2,128)S(1)}, s32[3,4,2]{1,2,0:T(2,128)}, u32[]{:S(2)}) copy-start(s32[3,4,2]{1,2,0:T(2,128)} %param.24) | copy-start | bytes 292
  4.1 5.2 %collective-permute-start.2 = (bf16[3,4,1152]{2,1,0:T(4,128)(2,1)S(1)}, bf16[3,4,1152]{2,1,0:T(4,128)(2,1)S(1)}, u32[]{:S(2)}, u32[]{:S(2)}) collective-permute-start(bf16[3,4,1152]{2,1,0:T(4,128)(2,1)S(1)} %get-tuple-element.15.refs_0_.refs_1_), channel_id=1, source_target_pairs={{0,24},{8,16},{16,8},{24,0},{1,25},{9,17},{17,9},{25,1},{2,26},{10... | collective-permute-start | bytes 82952 | tf_op jit(solution)/shard_map/ppermute | solution.py:449
  5.8 3.6 %collective-permute-start.1 = (bf16[3,4,1152]{2,1,0:T(4,128)(2,1)S(1)}, bf16[3,4,1152]{2,1,0:T(4,128)(2,1)S(1)}, u32[]{:S(2)}, u32[]{:S(2)}) collective-permute-start(bf16[3,4,1152]{2,1,0:T(4,128)(2,1)S(1)} %get-tuple-element.15.refs_0_.refs_1_), channel_id=1, source_target_pairs={{0,16},{8,24},{16,0},{24,8},{1,17},{9,25},{17,1},{25,9},{2,18},{10... | collective-permute-start | bytes 82952 | tf_op jit(solution)/shard_map/ppermute | solution.py:449
  6.0 3.3 %collective-permute-start = (bf16[3,4,1152]{2,1,0:T(4,128)(2,1)S(1)}, bf16[3,4,1152]{2,1,0:T(4,128)(2,1)S(1)}, u32[]{:S(2)}, u32[]{:S(2)}) collective-permute-start(bf16[3,4,1152]{2,1,0:T(4,128)(2,1)S(1)} %get-tuple-element.15.refs_0_.refs_1_), channel_id=1, source_target_pairs={{0,8},{8,0},{16,24},{24,16},{1,9},{9,1},{17,25},{25,17},{2,10},{10... | collective-permute-start | bytes 82952 | tf_op jit(solution)/shard_map/ppermute | solution.py:449
  10.7 8.0 %collective-permute-start.5 = (bf16[3,4,1152]{2,1,0:T(4,128)(2,1)S(1)}, bf16[3,4,1152]{2,1,0:T(4,128)(2,1)S(1)}, u32[]{:S(2)}, u32[]{:S(2)}) collective-permute-start(bf16[3,4,1152]{2,1,0:T(4,128)(2,1)S(1)} %get-tuple-element.18.refs_0_), channel_id=1, source_target_pairs={{0,6},{1,7},{2,4},{3,5},{4,2},{5,3},{6,0},{7,1},{8,14},{9,15},{10,... | collective-permute-start | bytes 82952 | tf_op jit(solution)/shard_map/ppermute | solution.py:449
  15.7 4.0 %collective-permute-start.4 = (bf16[3,4,1152]{2,1,0:T(4,128)(2,1)S(1)}, bf16[3,4,1152]{2,1,0:T(4,128)(2,1)S(1)}, u32[]{:S(2)}, u32[]{:S(2)}) collective-permute-start(bf16[3,4,1152]{2,1,0:T(4,128)(2,1)S(1)} %get-tuple-element.18.refs_0_), channel_id=1, source_target_pairs={{0,4},{1,5},{2,6},{3,7},{4,0},{5,1},{6,2},{7,3},{8,12},{9,13},{10,... | collective-permute-start | bytes 82952 | tf_op jit(solution)/shard_map/ppermute | solution.py:449
  15.7 4.0 %collective-permute-start.3 = (bf16[3,4,1152]{2,1,0:T(4,128)(2,1)S(1)}, bf16[3,4,1152]{2,1,0:T(4,128)(2,1)S(1)}, u32[]{:S(2)}, u32[]{:S(2)}) collective-permute-start(bf16[3,4,1152]{2,1,0:T(4,128)(2,1)S(1)} %get-tuple-element.18.refs_0_), channel_id=1, source_target_pairs={{0,2},{1,3},{2,0},{3,1},{4,6},{5,7},{6,4},{7,5},{8,10},{9,11},{10,... | collective-permute-start | bytes 82952 | tf_op jit(solution)/shard_map/ppermute | solution.py:449
  16.0 7.6 %copy-start = (bf16[1024,16]{0,1:T(8,128)(2,1)S(1)}, bf16[1024,16]{0,1:T(8,128)(2,1)}, u32[]{:S(2)}) copy-start(bf16[1024,16]{0,1:T(8,128)(2,1)} %param.23) | copy-start | bytes 98308
  19.8 3.8 %collective-permute-start.6 = (bf16[4,3,4,1152]{3,2,1,0:T(4,128)(2,1)S(1)}, bf16[4,3,4,1152]{3,2,1,0:T(4,128)(2,1)S(1)}, u32[]{:S(2)}, u32[]{:S(2)}) collective-permute-start(bf16[4,3,4,1152]{3,2,1,0:T(4,128)(2,1)S(1)} %pad_maximum_fusion.near_ref), channel_id=1, source_target_pairs={{0,1},{1,0},{2,3},{3,2},{4,5},{5,4},{6,7},{7,6},{8,9},{9,8},{10,11... | collective-permute-start | bytes 331784 | tf_op jit(solution)/shard_map/ppermute | solution.py:449

commit v2 on v0

--- a/solution.py
+++ b/solution.py
@@ -205,13 +205,10 @@
                 one(r, count)
 
 
-def project(count, columns, ids_ref, hidden_ref, gain_ref, weight_ref, *refs):
+def project(count, columns, ids_ref, hidden_ref, gain_ref, weight_ref, expand_ref, *refs):
     parts = refs[:count]
-    attn_ref, own_ref, send_ref, attn_buf, res_buf = refs[count:]
+    send_ref, attn_ref, res_ref = refs[count:]
     requests, steps, width = hidden_ref.shape
-    feature = attn_ref.shape[2]
-    head = width // HEADS
-    seq = lax.axis_index("seq")
     tp = lax.axis_index("tp")
 
     def moved(x, amount):
@@ -233,15 +230,10 @@
     real = (iota(total.shape, 1) < HEADS) & (iota(total.shape, 0) < requests * steps)
     inverse = jnp.where(real, 1.0 / jnp.where(real, total, 1.0), 0.0)
     ratio = jnp.concatenate([jnp.where(real, f, 0.0) * inverse for f in factors], axis=0)
-    expand = jnp.where(
-        (within(iota((LANES, width), 0), HEADS) == over(iota((LANES, width), 1), head))
-        & (iota((LANES, width), 0) < 3 * HEADS),
-        1.0,
-        0.0,
-    ).astype(jnp.bfloat16)
     hi, mid, low = three_parts(ratio)
     packed = hi + pltpu.roll(mid, HEADS, 1) + pltpu.roll(low, 2 * HEADS, 1)
-    wide = jnp.dot(packed.astype(jnp.bfloat16), expand, preferred_element_type=jnp.float32)
+    packed = packed.astype(jnp.bfloat16)[:, : 4 * HEADS]
+    wide = jnp.dot(packed, expand_ref[...], preferred_element_type=jnp.float32)
     context = jnp.zeros((ROWS, width), jnp.float32)
     for b, ref in enumerate(parts):
         context = context + wide[b * ROWS : (b + 1) * ROWS] * rows_of(ref, slice(0, width))
@@ -267,15 +259,8 @@
         [jnp.where(tail, extra, normed[:, :columns]), normed[:, columns:]], axis=1
     ).astype(jnp.bfloat16)
     send_ref[...] = message
-    attn_buf[...] = attention
-    res_buf[...] = residual
-    lanes = pl.ds(pl.multiple_of(seq * feature, feature), feature)
-    mine = attn_buf[:, lanes]
-    for r in range(requests):
-        attn_ref[r] = mine[r * steps : (r + 1) * steps].astype(jnp.bfloat16)
-    rest = res_buf[:, lanes]
-    for r in range(requests):
-        own_ref[r] = rest[r * steps : (r + 1) * steps]
+    attn_ref[...] = attention
+    res_ref[...] = residual
 
 
 def feed(
@@ -351,37 +336,61 @@
     return pltpu.CompilerParams(vmem_limit_bytes=mebibytes * 1024 * 1024)
 
 
-def stage(count, *refs):
-    sources, copies, sems = refs[1 : 1 + count], refs[1 + count : 1 + 2 * count], refs[-1]
+def stage(count, beside, extras, *refs):
+    sources, rest = refs[:count], refs[count:]
+    inputs, copies = rest[:extras], rest[extras : extras + count]
+    sems, others = rest[-1], rest[extras + count : -1]
     moves = [
         pltpu.make_async_copy(source, copy, sems.at[i])
         for i, (source, copy) in enumerate(zip(sources, copies))
     ]
     for move in moves:
         move.start()
+    beside(inputs, others, sems.at[count])
     for move in moves:
         move.wait()
 
 
-def staged(after, *arrays, result=None):
+def spread_heads(inputs, others, sem):
+    expand_ref = others[0]
+    shape = expand_ref.shape
+    head = shape[1] // HEADS
+    row = iota(shape, 0)
+    same = (within(row, HEADS) == over(iota(shape, 1), head)) & (row < 3 * HEADS)
+    expand_ref[...] = jnp.where(same, 1.0, 0.0).astype(jnp.bfloat16)
+
+
+def own_features(inputs, others, sem):
+    attn_ref, res_ref = inputs
+    attn_hbm, own_ref, attn_buf = others
+    requests, steps, feature = own_ref.shape
+    seq = lax.axis_index("seq")
+    lanes = pl.ds(pl.multiple_of(seq * feature, feature), feature)
+    attention, residual = attn_ref[:, lanes], res_ref[:, lanes]
+    for r in range(requests):
+        part = slice(r * steps, (r + 1) * steps)
+        attn_buf[r] = attention[part].astype(jnp.bfloat16)
+        own_ref[r] = residual[part]
+    move = pltpu.make_async_copy(attn_buf, attn_hbm, sem)
+    move.start()
+    move.wait()
+
+
+def staged(beside, arrays, extras, shapes, specs, scratch=()):
     anywhere = pl.BlockSpec(memory_space=pl.ANY)
-    inputs = [pltpu.with_memory_space_constraint(x, pltpu.HBM) for x in arrays]
-    shapes = [pltpu.VMEM(x.shape, x.dtype) for x in arrays]
-    if result is not None:
-        inputs.append(result)
-        shapes.append(pltpu.HBM(result.shape, result.dtype))
-    count = len(inputs)
+    vmem = pl.BlockSpec(memory_space=pltpu.VMEM)
+    count = len(arrays)
     size = sum(2 * x.size for x in arrays)
     return pl.pallas_call(
-        functools.partial(stage, count),
-        out_shape=tuple(shapes),
-        in_specs=[anywhere] * (1 + count),
-        out_specs=(anywhere,) * count,
-        scratch_shapes=[pltpu.SemaphoreType.DMA((count,))],
+        functools.partial(stage, count, beside, len(extras)),
+        out_shape=tuple(pltpu.VMEM(x.shape, x.dtype) for x in arrays) + tuple(shapes),
+        in_specs=[anywhere] * count + [vmem] * len(extras),
+        out_specs=(anywhere,) * count + tuple(specs),
+        scratch_shapes=list(scratch) + [pltpu.SemaphoreType.DMA((count + 1,))],
         compiler_params=limit(4),
         cost_estimate=pl.CostEstimate(flops=0, bytes_accessed=2 * size, transcendentals=0),
         name="stage",
-    )(after, *inputs)
+    )(*[pltpu.with_memory_space_constraint(x, pltpu.HBM) for x in arrays], *extras)
 
 
 def body(
@@ -443,25 +452,39 @@
     def swapped(x, axis, size, d):
         return lax.ppermute(x, axis, [(i, i ^ d) for i in range(size)])
 
-    out_weight, gate_weight = staged(part, out_weight, gate_weight)
+    out_weight, gate_weight, expand = staged(
+        spread_heads,
+        (out_weight, gate_weight),
+        (part,),
+        (pltpu.VMEM((4 * HEADS, width), jnp.bfloat16),),
+        (vmem,),
+    )
     parts = [fresh, part] + [swapped(part, "seq", seq_size, d) for d in range(1, seq_size)]
-    attn_out, own_residual, packed = pl.pallas_call(
+    row_sums = pltpu.VMEM((ROWS, width), jnp.float32)
+    packed, attention, residual = pl.pallas_call(
         functools.partial(project, seq_size + 1, tp_size * ROWS),
-        out_shape=(
-            pltpu.VMEM((requests, steps, feature), jnp.bfloat16),
-            jax.ShapeDtypeStruct((requests, steps, feature), jnp.float32),
-            jax.ShapeDtypeStruct((ROWS, width), jnp.bfloat16),
-        ),
-        in_specs=[smem] + [vmem] * (4 + seq_size),
+        out_shape=(pltpu.VMEM((ROWS, width), jnp.bfloat16), row_sums, row_sums),
+        in_specs=[smem] + [vmem] * (5 + seq_size),
         out_specs=(vmem, vmem, vmem),
-        scratch_shapes=[
-            pltpu.VMEM((ROWS, width), jnp.float32),
-            pltpu.VMEM((ROWS, width), jnp.float32),
-        ],
         compiler_params=limit(8),
         name="project",
-    )(expert_ids.transpose(0, 2, 1), hidden_in, norm_gain.reshape(1, width), out_weight, *parts)
-    up_weight, down_weight, attn_out = staged(packed, up_weight, down_weight, result=attn_out)
+    )(
+        expert_ids.transpose(0, 2, 1),
+        hidden_in,
+        norm_gain.reshape(1, width),
+        out_weight,
+        expand,
+        *parts,
+    )
+    own = (requests, steps, feature)
+    up_weight, down_weight, attn_out, own_residual = staged(
+        own_features,
+        (up_weight, down_weight),
+        (attention, residual),
+        (pltpu.HBM(own, jnp.bfloat16), pltpu.VMEM(own, jnp.float32)),
+        (pl.BlockSpec(memory_space=pl.ANY), vmem),
+        (pltpu.VMEM(own, jnp.bfloat16),),
+    )
     near = jnp.stack(
         [packed] + [swapped(packed, "tp", tp_size, 2 * d) for d in range(1, tp_size // 2)]
     )

time: 39.3 us -> 39.5 us (level); the launches traced: 39.7 us -> 38.8 us
  Pallas kernels: 14 us -> 12.4 us
  starting transfers between devices: 9.85 us -> 10.6 us
    pallas_call x1, Pallas kernels: 5.03 us -> 3.44 us  [body(): pl.pallas_call(attend, out_shape=(partial, partial), in_specs=[hbm] * 6,...]
    ppermute x7, starting transfers between devices: 9.85 us -> 10.6 us  [swapped(): return lax.ppermute(x, axis, [(i, i ^ d) for i in range(size)])]
  transfers between devices with their start and end apart: 7 -> 7, of which waited for: 3 -> 2; matrix products, arithmetic and copies ran while one was open for 0% -> 0% of each run, Pallas kernels for 13% -> 13%
where the time goes in v2:
time: 39.5 us; the launch traced here: 38.8 us
  blocking collectives  12.7 us (32%)
  Pallas kernels  12.4 us (31%)
  starting transfers between devices  10.6 us (27%)
  waiting for transfers between devices  1.57 us (4%)
  between operations  0.76 us (2%)
  other arithmetic  0.72 us (2%)
    all_to_all x1, blocking collectives, body(): arrived = lax.all_to_all(terms, ('seq', 'tp'), 0, 0, tiled=True)  12.7 us
    ppermute x7, starting transfers between devices, swapped(): return lax.ppermute(x, axis, [(i, i ^ d) for i in range(size)])  10.6 us
    pallas_call x2, Pallas kernels, staged(): pl.pallas_call(functools.partial(stage, count, beside, len(extras)), out_...  5.19 us
    pallas_call x1, Pallas kernels, body(): pl.pallas_call(attend, out_shape=(partial, partial), in_specs=[hbm] * 6,...  3.44 us
    pallas_call x1, Pallas kernels, body(): pl.pallas_call(functools.partial(feed, capacity, steps, requests * steps,...  2.43 us
    ppermute x7, waiting for transfers between devices, swapped(): return lax.ppermute(x, axis, [(i, i ^ d) for i in range(size)])  1.57 us
    pallas_call x1, Pallas kernels, body(): pl.pallas_call(functools.partial(project, seq_size + 1, tp_size * ROWS),...  1.37 us
  transfers between devices with their start and end apart: 7, of which 2 were waited for; matrix products, arithmetic and copies ran while one was open for 0% of the time, Pallas kernels for 13%

profile of v2, /device:TPU:1, one launch (start us, length us, event | category | flops | bytes accessed | tf_op | source)
XLA Modules:
  0.0 38.8 jit_solution(9450388800742531678)
XLA Ops:
  0.6 3.4 %attend.1 = (bf16[3,4,1152]{2,1,0:T(4,128)(2,1)S(1)}, bf16[3,4,1152]{2,1,0:T(4,128)(2,1)S(1)}) custom-call(s32[3]{0:T(128)} %lens_hbm.1, bf16[3,4,1024]{2,1,0:T(4,128)(2,1)} %q_hbm.1, bf16[3,4,1024]{2,1,0:T(4,128)(2,1)} %nk_hbm.1, bf16[3,4,1024]{2,1,0:T(4,128)(2,1)} %nv_hbm.1, bf16[3,1024,1024]{2,1,0:T(8,128)(2,1)} %k_hbm.1, bf16[3,1024,1024]{2,1,0:T(8,128)(2,1)} %v_hbm.1), custom_call_target="tpu_custom_call" | custom-call | tf_op jit(solution)/shard_map/attend/pallas_call | solution.py:427
  4.1 0.0 copy-start.1
  4.1 0.0 copy-start.2
  4.1 0.0 copy-start.3
  4.1 1.6 %collective-permute-start.2 = (bf16[3,4,1152]{2,1,0:T(4,128)(2,1)S(1)}, bf16[3,4,1152]{2,1,0:T(4,128)(2,1)S(1)}, u32[]{:S(2)}, u32[]{:S(2)}) collective-permute-start(bf16[3,4,1152]{2,1,0:T(4,128)(2,1)S(1)} %get-tuple-element.17.refs_2_.refs_1_), channel_id=1, source_target_pairs={{0,24},{8,16},{16,8},{24,0},{1,25},{9,17},{17,9},{25,1},{2,26},{10... | collective-permute-start | bytes 82952 | tf_op jit(solution)/shard_map/ppermute | solution.py:453
  5.8 0.2 collective-permute-start.1
  6.0 0.8 %collective-permute-start = (bf16[3,4,1152]{2,1,0:T(4,128)(2,1)S(1)}, bf16[3,4,1152]{2,1,0:T(4,128)(2,1)S(1)}, u32[]{:S(2)}, u32[]{:S(2)}) collective-permute-start(bf16[3,4,1152]{2,1,0:T(4,128)(2,1)S(1)} %get-tuple-element.17.refs_2_.refs_1_), channel_id=1, source_target_pairs={{0,8},{8,0},{16,24},{24,16},{1,9},{9,1},{17,25},{25,17},{2,10},{10... | collective-permute-start | bytes 82952 | tf_op jit(solution)/shard_map/ppermute | solution.py:453
  6.8 2.5 %stage.2 = (bf16[1024,1024]{1,0:T(8,128)(2,1)S(1)}, bf16[1408,1024]{1,0:T(8,128)(2,1)S(1)}, bf16[64,1024]{1,0:T(8,128)(2,1)S(1)}) custom-call(bf16[1024,1024]{1,0:T(8,128)(2,1)} %refs_0_.2, bf16[1408,1024]{1,0:T(8,128)(2,1)} %refs_1_.2, bf16[3,4,1152]{2,1,0:T(4,128)(2,1)S(1)} %get-tuple-element.17.refs_2_.refs_1_), custom_call_target="tpu_custom_call" | custom-call | bytes 9961472 | tf_op jit(solution)/shard_map/stage/pallas_call | solution.py:384
  9.3 0.0 collective-permute-done.2.refs_4_
  9.3 0.0 collective-permute-done.1.refs_3_
  9.3 0.0 collective-permute-done.refs_2_
  9.3 0.0 copy-done.1
  9.3 0.0 copy-done.2
  9.4 0.0 copy-done.3
  9.4 1.4 %project.1 = (bf16[16,1024]{1,0:T(8,128)(2,1)S(1)}, f32[16,1024]{1,0:T(8,128)S(1)}, f32[16,1024]{1,0:T(8,128)S(1)}) custom-call(s32[3,2,4]{2,1,0:T(2,128)S(1)} %bitcast.12, bf16[3,4,1024]{2,1,0:T(4,128)(2,1)S(1)} %copy-done.1, f32[1,1024]{1,0:T(1,128)S(1)} %bitcast.11, bf16[1024,1024]{1,0:T(8,128)(2,1)S(1)} %get-tuple-element.18.weight_ref, ...), custom_call_target="tpu_custom_call" | custom-call | tf_op jit(solution)/shard_map/project/pallas_call | solution.py:464
  10.8 5.8 %collective-permute-start.5 = (bf16[16,1024]{1,0:T(8,128)(2,1)S(1)}, bf16[16,1024]{1,0:T(8,128)(2,1)S(1)}, u32[]{:S(2)}, u32[]{:S(2)}) collective-permute-start(bf16[16,1024]{1,0:T(8,128)(2,1)S(1)} %get-tuple-element.26), channel_id=1, source_target_pairs={{0,6},{1,7},{2,4},{3,5},{4,2},{5,3},{6,0},{7,1},{8,14},{9,15},{10,... | collective-permute-start | bytes 98312 | tf_op jit(solution)/shard_map/ppermute | solution.py:453
  16.6 0.0 collective-permute-start.4
  16.6 0.4 collective-permute-start.3
  16.9 0.0 copy-start
  16.9 2.7 %stage.3 = (bf16[1408,1024]{1,0:T(8,128)(2,1)S(1)}, bf16[1408,1024]{1,0:T(8,128)(2,1)S(1)}, bf16[3,4,256]{2,1,0:T(4,128)(2,1)}, f32[3,4,256]{2,1,0:T(4,128)S(1)}) custom-call(bf16[1408,1024]{1,0:T(8,128)(2,1)} %refs_0_.3, bf16[1408,1024]{1,0:T(8,128)(2,1)} %refs_1_.3, f32[16,1024]{1,0:T(8,128)S(1)} %get-tuple-element.21.refs_2_, ...), custom_call_target="tpu_custom_call" | custom-call | bytes 11534336 | tf_op jit(solution)/shard_map/stage/pallas_call | solution.py:384
  19.7 0.0 collective-permute-done.5
  19.7 0.6 %collective-permute-done.4 = bf16[16,1024]{1,0:T(8,128)(2,1)S(1)} collective-permute-done((bf16[16,1024]{1,0:T(8,128)(2,1)S(1)}, bf16[16,1024]{1,0:T(8,128)(2,1)S(1)}, u32[]{:S(2)}, u32[]{:S(2)}) %collective-permute-start.4) | collective-permute-done | bytes 32800 | tf_op jit(solution)/shard_map/ppermute | solution.py:453
  20.2 0.0 collective-permute-done.3
  20.3 1.7 %collective-permute-start.6 = (bf16[4,16,1024]{2,1,0:T(8,128)(2,1)S(1)}, bf16[4,16,1024]{2,1,0:T(8,128)(2,1)S(1)}, u32[]{:S(2)}, u32[]{:S(2)}) collective-permute-start(bf16[4,16,1024]{2,1,0:T(8,128)(2,1)S(1)} %pad_maximum_fusion.near_ref), channel_id=1, source_target_pairs={{0,1},{1,0},{2,3},{3,2},{4,5},{5,4},{6,7},{7,6},{8,9},{9,8},{10,11... | collective-permute-start | bytes 393224 | tf_op jit(solution)/shard_map/ppermute | solution.py:453
  22.0 1.0 %collective-permute-done.6.far_ref = bf16[4,16,1024]{2,1,0:T(8,128)(2,1)S(1)} collective-permute-done((bf16[4,16,1024]{2,1,0:T(8,128)(2,1)S(1)}, bf16[4,16,1024]{2,1,0:T(8,128)(2,1)S(1)}, u32[]{:S(2)}, u32[]{:S(2)}) %collective-permute-start.6) | collective-permute-done | bytes 131104 | tf_op jit(solution)/shard_map/ppermute | solution.py:453
  22.9 0.0 copy-done
  22.9 2.4 %feed.1 = bf16[4,8,3,4,256]{4,3,2,1,0:T(4,128)(2,1)S(1)} custom-call(bf16[16,1024]{1,0:T(8,128)(2,1)S(1)} %bitcast.9, bf16[1408,1024]{1,0:T(8,128)(2,1)S(1)} %get-tuple-element.25.gate_ref, bf16[1408,1024]{1,0:T(8,128)(2,1)S(1)} %get-tuple-element.29.up_ref, bf16[1408,1024]{1,0:T(8,128)(2,1)S(1)} %get-tuple-element.30.down_ref, ...), custom_call_target="tpu_custom_call" | custom-call | tf_op jit(solution)/shard_map/feed/pallas_call | solution.py:493
  25.4 12.7 %all_to_all.5 = bf16[32,3,4,256]{3,2,1,0:T(4,128)(2,1)S(1)} all-to-all(bf16[32,3,4,256]{3,2,1,0:T(4,128)(2,1)S(1)} %bitcast.8), channel_id=1, replica_groups=mesh['seq'=4,'tp'=8] {'seq','tp'}, dimensions={0} | all-to-all | bytes 393216 | tf_op jit(solution)/shard_map/all_to_all | solution.py:503
  38.1 0.1 convert_reduce_fusion
  38.2 0.6 %add_convert_fusion = bf16[3,4,256]{2,1,0:T(4,128)(2,1)} fusion(f32[3,4,256]{2,1,0:T(4,128)S(1)} %get-tuple-element.24, f32[3,4,256]{2,1,0:T(4,128)S(1)} %convert_reduce_fusion), kind=kLoop, calls=%fused_computation.2 | loop fusion | flops 6144 | bytes 30720 | tf_op jit(solution)/shard_map/convert_element_type | solution.py:505
  (1 shorter events, 0.0 us)
Async XLA Ops:
  4.1 5.3 %copy-start.1 = (bf16[3,4,1024]{2,1,0:T(4,128)(2,1)S(1)}, bf16[3,4,1024]{2,1,0:T(4,128)(2,1)}, u32[]{:S(2)}) copy-start(bf16[3,4,1024]{2,1,0:T(4,128)(2,1)} %hidden_ref.1) | copy-start | bytes 73732
  4.1 5.3 %copy-start.2 = (f32[1024]{0:T(1024)S(1)}, f32[1024]{0:T(1024)}, u32[]{:S(2)}) copy-start(f32[1024]{0:T(1024)} %param.22) | copy-start | bytes 12292
  4.1 5.3 %copy-start.3 = (s32[3,4,2]{1,2,0:T(2,128)S(1)}, s32[3,4,2]{1,2,0:T(2,128)}, u32[]{:S(2)}) copy-start(s32[3,4,2]{1,2,0:T(2,128)} %param.24) | copy-start | bytes 292
  4.1 5.2 %collective-permute-start.2 = (bf16[3,4,1152]{2,1,0:T(4,128)(2,1)S(1)}, bf16[3,4,1152]{2,1,0:T(4,128)(2,1)S(1)}, u32[]{:S(2)}, u32[]{:S(2)}) collective-permute-start(bf16[3,4,1152]{2,1,0:T(4,128)(2,1)S(1)} %get-tuple-element.17.refs_2_.refs_1_), channel_id=1, source_target_pairs={{0,24},{8,16},{16,8},{24,0},{1,25},{9,17},{17,9},{25,1},{2,26},{10... | collective-permute-start | bytes 82952 | tf_op jit(solution)/shard_map/ppermute | solution.py:453
  5.8 3.6 %collective-permute-start.1 = (bf16[3,4,1152]{2,1,0:T(4,128)(2,1)S(1)}, bf16[3,4,1152]{2,1,0:T(4,128)(2,1)S(1)}, u32[]{:S(2)}, u32[]{:S(2)}) collective-permute-start(bf16[3,4,1152]{2,1,0:T(4,128)(2,1)S(1)} %get-tuple-element.17.refs_2_.refs_1_), channel_id=1, source_target_pairs={{0,16},{8,24},{16,0},{24,8},{1,17},{9,25},{17,1},{25,9},{2,18},{10... | collective-permute-start | bytes 82952 | tf_op jit(solution)/shard_map/ppermute | solution.py:453
  6.0 3.3 %collective-permute-start = (bf16[3,4,1152]{2,1,0:T(4,128)(2,1)S(1)}, bf16[3,4,1152]{2,1,0:T(4,128)(2,1)S(1)}, u32[]{:S(2)}, u32[]{:S(2)}) collective-permute-start(bf16[3,4,1152]{2,1,0:T(4,128)(2,1)S(1)} %get-tuple-element.17.refs_2_.refs_1_), channel_id=1, source_target_pairs={{0,8},{8,0},{16,24},{24,16},{1,9},{9,1},{17,25},{25,17},{2,10},{10... | collective-permute-start | bytes 82952 | tf_op jit(solution)/shard_map/ppermute | solution.py:453
  10.8 8.9 %collective-permute-start.5 = (bf16[16,1024]{1,0:T(8,128)(2,1)S(1)}, bf16[16,1024]{1,0:T(8,128)(2,1)S(1)}, u32[]{:S(2)}, u32[]{:S(2)}) collective-permute-start(bf16[16,1024]{1,0:T(8,128)(2,1)S(1)} %get-tuple-element.26), channel_id=1, source_target_pairs={{0,6},{1,7},{2,4},{3,5},{4,2},{5,3},{6,0},{7,1},{8,14},{9,15},{10,... | collective-permute-start | bytes 98312 | tf_op jit(solution)/shard_map/ppermute | solution.py:453
  16.6 3.7 %collective-permute-start.4 = (bf16[16,1024]{1,0:T(8,128)(2,1)S(1)}, bf16[16,1024]{1,0:T(8,128)(2,1)S(1)}, u32[]{:S(2)}, u32[]{:S(2)}) collective-permute-start(bf16[16,1024]{1,0:T(8,128)(2,1)S(1)} %get-tuple-element.26), channel_id=1, source_target_pairs={{0,4},{1,5},{2,6},{3,7},{4,0},{5,1},{6,2},{7,3},{8,12},{9,13},{10,... | collective-permute-start | bytes 98312 | tf_op jit(solution)/shard_map/ppermute | solution.py:453
  16.6 3.7 %collective-permute-start.3 = (bf16[16,1024]{1,0:T(8,128)(2,1)S(1)}, bf16[16,1024]{1,0:T(8,128)(2,1)S(1)}, u32[]{:S(2)}, u32[]{:S(2)}) collective-permute-start(bf16[16,1024]{1,0:T(8,128)(2,1)S(1)} %get-tuple-element.26), channel_id=1, source_target_pairs={{0,2},{1,3},{2,0},{3,1},{4,6},{5,7},{6,4},{7,5},{8,10},{9,11},{10,... | collective-permute-start | bytes 98312 | tf_op jit(solution)/shard_map/ppermute | solution.py:453
  16.9 6.0 %copy-start = (bf16[1024,16]{0,1:T(8,128)(2,1)S(1)}, bf16[1024,16]{0,1:T(8,128)(2,1)}, u32[]{:S(2)}) copy-start(bf16[1024,16]{0,1:T(8,128)(2,1)} %param.23) | copy-start | bytes 98308
  20.3 2.7 %collective-permute-start.6 = (bf16[4,16,1024]{2,1,0:T(8,128)(2,1)S(1)}, bf16[4,16,1024]{2,1,0:T(8,128)(2,1)S(1)}, u32[]{:S(2)}, u32[]{:S(2)}) collective-permute-start(bf16[4,16,1024]{2,1,0:T(8,128)(2,1)S(1)} %pad_maximum_fusion.near_ref), channel_id=1, source_target_pairs={{0,1},{1,0},{2,3},{3,2},{4,5},{5,4},{6,7},{7,6},{8,9},{9,8},{10,11... | collective-permute-start | bytes 393224 | tf_op jit(solution)/shard_map/ppermute | solution.py:453
